TPU v7x, 512 devices: a whole 4x4x16 slice. The times are simulated.
512 devices in a mesh: dp: 64 (over z, y), seq: 8 (over x, core).
Axes of the slice: x: 4, y: 4, z: 16, core: 2. Of those that a mesh axis runs over, the one named last changes fastest.
Arguments:
- queries: bfloat16 [65536, 1024], P(('dp', 'seq')), may hold values from -2.5 to 2.5
- key_vectors: bfloat16 [65536, 1024], P(('dp', 'seq')), may hold values from -2.5 to 2.5
- value_vectors: bfloat16 [65536, 1024], P(('dp', 'seq')), may hold values from -6 to 6
- gate_vectors: bfloat16 [65536, 1024], P(('dp', 'seq')), may hold values from -6 to 6
- out_grad: float32 [65536, 1024], P(('dp', 'seq')), may hold values from -24 to 24
- out_weight: float32 [1024, 1024], P('dp'), may hold values from -0.1875 to 0.1875
- time_bias: bfloat16 [128, 8], replicated, may hold values from -3 to 3
- lengths: int32 [64, 4], P('dp'), may hold values from 1 to 512, 1024 in all within a row
- stamps: int32 [65536], P(('dp', 'seq')), may hold values from 0 to 255, as said below
Outputs:
- query_grad: bfloat16 [65536, 1024], P(('dp', 'seq'))
- key_grad: bfloat16 [65536, 1024], P(('dp', 'seq'))
- value_grad: bfloat16 [65536, 1024], P(('dp', 'seq'))
- gate_grad: bfloat16 [65536, 1024], P(('dp', 'seq'))
- weight_grad: float32 [1024, 1024], P('dp')
Inputs may be any that keep to these rules, and one draw needn't show every extreme that they name: Within each pack the stamps never fall from one event to the next; every pack has a first stamp of 0 and a last of 255. Each pack's 4 lengths sum to 1024, and the longest is exactly 512.
All inputs are finite; a program needn't handle non-finite values.
Results may differ from a plain program's by a relative error of at most 0.02.
Values may be sent and summed in bfloat16 or wider, within the bound.
A program may use at most 128 MiB of HBM per device.

v0:
```python
import math

import jax
import jax.numpy as jnp
from jax import lax
from jax.sharding import PartitionSpec as P

norm_eps = 1e-06
exact = lax.Precision.HIGHEST


def silu_slope(scores):
    sigma = jax.nn.sigmoid(scores)
    return sigma * (1.0 + scores * (1.0 - sigma))


def segment_of(places, seq_lengths):
    ends = jnp.cumsum(seq_lengths, dtype=jnp.int32)
    return jnp.sum((places[:, None] >= ends[None, :]).astype(jnp.int32), axis=1, dtype=jnp.int32)


def stamp_marks(stamps, stamp_span):
    return (stamps[:, None] == jnp.arange(stamp_span, dtype=jnp.int32)[None, :]).astype(
        jnp.bfloat16
    )


def stamp_table(time_bias, stamp_span):
    buckets, heads = time_bias.shape
    farther = jnp.concatenate(
        [time_bias[1:], jnp.broadcast_to(time_bias[buckets - 1 :], (stamp_span - buckets, heads))],
        axis=0,
    )
    cyclic = jnp.concatenate(
        [jnp.broadcast_to(time_bias[:1], (stamp_span, heads)), farther[::-1]], axis=0
    )
    tiled = jnp.tile(cyclic, (stamp_span, 1))[: stamp_span * (2 * stamp_span - 2)]
    return tiled.reshape(stamp_span, 2 * stamp_span - 2, heads)[:, :stamp_span, :]


def split_heads(block, heads):
    return block.reshape(block.shape[0], heads, block.shape[1] // heads)


def allowed_pairs(query_place, query_segment, key_place, key_segment):
    return (query_segment[:, None] == key_segment[None, :]) & (
        key_place[None, :] <= query_place[:, None]
    )


def tile_scores(query_tile, key_tile, bias, heads):
    raw_scores = jnp.einsum(
        "qhd,khd->hqk",
        split_heads(query_tile, heads),
        split_heads(key_tile, heads),
        preferred_element_type=jnp.float32,
    )
    return raw_scores + bias


def tile_forward(query_tile, key_tile, value_tile, bias, allowed, heads):
    scores = tile_scores(query_tile, key_tile, bias, heads)
    probs = jnp.where(allowed[None], jax.nn.silu(scores), 0.0).astype(jnp.bfloat16)
    mixed = jnp.einsum(
        "hqk,khd->qhd", probs, split_heads(value_tile, heads), preferred_element_type=jnp.float32
    )
    return mixed.reshape(mixed.shape[0], -1)


def tile_query_grad(query_tile, key_tile, value_tile, upstream, bias, allowed, heads):
    scores = tile_scores(query_tile, key_tile, bias, heads)
    prob_grad = jnp.einsum(
        "qhd,khd->hqk",
        split_heads(upstream, heads),
        split_heads(value_tile, heads),
        preferred_element_type=jnp.float32,
    )
    score_grad = jnp.where(allowed[None], prob_grad * silu_slope(scores), 0.0).astype(jnp.bfloat16)
    mixed = jnp.einsum(
        "hqk,khd->qhd", score_grad, split_heads(key_tile, heads), preferred_element_type=jnp.float32
    )
    return mixed.reshape(mixed.shape[0], -1)


def tile_key_grad(query_tile, upstream, key_tile, value_tile, bias, allowed, heads):
    scores = tile_scores(query_tile, key_tile, bias, heads)
    probs = jnp.where(allowed[None], jax.nn.silu(scores), 0.0).astype(jnp.bfloat16)
    upstream_heads = split_heads(upstream, heads)
    prob_grad = jnp.einsum(
        "qhd,khd->hqk",
        upstream_heads,
        split_heads(value_tile, heads),
        preferred_element_type=jnp.float32,
    )
    score_grad = jnp.where(allowed[None], prob_grad * silu_slope(scores), 0.0).astype(jnp.bfloat16)
    key_part = jnp.einsum(
        "hqk,qhd->khd",
        score_grad,
        split_heads(query_tile, heads),
        preferred_element_type=jnp.float32,
    )
    value_part = jnp.einsum(
        "hqk,qhd->khd", probs, upstream_heads, preferred_element_type=jnp.float32
    )
    return (key_part.reshape(key_part.shape[0], -1), value_part.reshape(value_part.shape[0], -1))


def shards(
    queries,
    key_vectors,
    value_vectors,
    gate_vectors,
    out_grad,
    out_weight,
    time_bias,
    lengths,
    stamps,
):
    row_count, width = queries.shape
    heads = time_bias.shape[1]
    stamp_span = 2 * time_bias.shape[0]
    seq_here = lax.axis_index("seq")
    seq_lengths = lengths[0]
    local_rows = jnp.arange(row_count, dtype=jnp.int32)
    table = stamp_table(time_bias, stamp_span)
    pack_keys, pack_values, pack_stamps = (
        lax.all_gather(key_vectors, "seq", axis=0, tiled=True),
        lax.all_gather(value_vectors, "seq", axis=0, tiled=True),
        lax.all_gather(stamps, "seq", axis=0, tiled=True),
    )
    slot_count = pack_keys.shape[0]
    key_place = jnp.arange(slot_count, dtype=jnp.int32)
    key_segment = segment_of(key_place, seq_lengths)
    key_marks = stamp_marks(pack_stamps, stamp_span)
    key_block = math.gcd(slot_count, 256)
    query_place = seq_here * row_count + local_rows
    query_stamps = jnp.take(pack_stamps, query_place)
    query_segment = segment_of(query_place, seq_lengths)
    query_side = jnp.einsum(
        "qs,sth->qth",
        stamp_marks(query_stamps, stamp_span),
        table,
        preferred_element_type=jnp.float32,
    ).astype(jnp.bfloat16)

    def sweep_keys(tile_fn):

        def sweep_step(index, total):
            begin = index * key_block
            key_tile = lax.dynamic_slice_in_dim(pack_keys, begin, key_block, 0)
            value_tile = lax.dynamic_slice_in_dim(pack_values, begin, key_block, 0)
            tile_place = lax.dynamic_slice_in_dim(key_place, begin, key_block, 0)
            tile_segment = lax.dynamic_slice_in_dim(key_segment, begin, key_block, 0)
            tile_marks = lax.dynamic_slice_in_dim(key_marks, begin, key_block, 0)
            allowed = allowed_pairs(query_place, query_segment, tile_place, tile_segment)

            def sweep_compute():
                bias = jnp.einsum(
                    "qth,kt->hqk", query_side, tile_marks, preferred_element_type=jnp.float32
                )
                return tile_fn(key_tile, value_tile, bias, allowed)

            return total + lax.cond(
                jnp.any(allowed), sweep_compute, lambda: jnp.zeros((row_count, width), jnp.float32)
            )

        return lax.fori_loop(
            0, slot_count // key_block, sweep_step, jnp.zeros((row_count, width), jnp.float32)
        )

    def forward_tile(key_tile, value_tile, bias, allowed):
        return tile_forward(queries, key_tile, value_tile, bias, allowed, heads)

    attended = sweep_keys(forward_tile)
    centred = attended - jnp.mean(attended, axis=1, keepdims=True)
    inverse_scale = lax.rsqrt(jnp.mean(centred * centred, axis=1, keepdims=True) + norm_eps)
    normed = centred * inverse_scale
    gate_float = gate_vectors.astype(jnp.float32)
    gated = normed * gate_float
    columns = out_grad
    gated_grad = jnp.dot(
        columns,
        lax.all_gather(out_weight.astype(jnp.bfloat16), "dp", axis=0, tiled=True).astype(
            jnp.float32
        ),
        precision=exact,
        preferred_element_type=jnp.float32,
    )
    columns = out_grad
    share = lax.psum_scatter(
        lax.dot_general(
            columns,
            gated,
            (((0,), (0,)), ((), ())),
            precision=exact,
            preferred_element_type=jnp.float32,
        ),
        "dp",
        scatter_dimension=0,
        tiled=True,
    )
    weight_total = lax.psum(share.astype(jnp.bfloat16), "seq").astype(jnp.float32)
    weight_grad = weight_total / row_count
    gate_grad = (gated_grad * normed).astype(jnp.bfloat16)
    normed_grad = gated_grad * gate_float
    attended_grad = (
        inverse_scale
        * (
            normed_grad
            - jnp.mean(normed_grad, axis=1, keepdims=True)
            - normed * jnp.mean(normed_grad * normed, axis=1, keepdims=True)
        )
    ).astype(jnp.bfloat16)

    def query_tile_grad(key_tile, value_tile, bias, allowed):
        return tile_query_grad(queries, key_tile, value_tile, attended_grad, bias, allowed, heads)

    query_grad = sweep_keys(query_tile_grad).astype(jnp.bfloat16)
    own_place = seq_here * row_count + local_rows
    own_segment = segment_of(own_place, seq_lengths)
    key_side = jnp.einsum(
        "sth,kt->skh", table, stamp_marks(stamps, stamp_span), preferred_element_type=jnp.float32
    ).astype(jnp.bfloat16)
    blank = jnp.zeros((row_count, width), jnp.float32)
    piece_rows = lax.all_gather(queries, "seq", axis=0, tiled=True)
    piece_grad = lax.all_gather(attended_grad, "seq", axis=0, tiled=True)
    piece_place = lax.all_gather(query_place, "seq", axis=0, tiled=True)
    piece_stamps = lax.all_gather(query_stamps, "seq", axis=0, tiled=True)
    piece_segment = segment_of(piece_place, seq_lengths)
    piece_marks = stamp_marks(piece_stamps, stamp_span)
    tile_size = math.gcd(piece_rows.shape[0], 256)

    def fold_step(index, sums):
        begin = index * tile_size
        query_tile = lax.dynamic_slice_in_dim(piece_rows, begin, tile_size, 0)
        upstream = lax.dynamic_slice_in_dim(piece_grad, begin, tile_size, 0)
        tile_place = lax.dynamic_slice_in_dim(piece_place, begin, tile_size, 0)
        tile_segment = lax.dynamic_slice_in_dim(piece_segment, begin, tile_size, 0)
        tile_marks = lax.dynamic_slice_in_dim(piece_marks, begin, tile_size, 0)
        allowed = allowed_pairs(tile_place, tile_segment, own_place, own_segment)

        def fold_compute():
            bias = jnp.einsum(
                "qs,skh->hqk", tile_marks, key_side, preferred_element_type=jnp.float32
            )
            return tile_key_grad(
                query_tile, upstream, key_vectors, value_vectors, bias, allowed, heads
            )

        empty = jnp.zeros((row_count, width), jnp.float32)
        key_part, value_part = lax.cond(jnp.any(allowed), fold_compute, lambda: (empty, empty))
        return (sums[0] + key_part, sums[1] + value_part)

    key_total, value_total = lax.fori_loop(
        0, piece_rows.shape[0] // tile_size, fold_step, (blank, blank)
    )
    return (
        query_grad,
        key_total.astype(jnp.bfloat16),
        value_total.astype(jnp.bfloat16),
        gate_grad,
        weight_grad,
    )


def solution(mesh):
    return jax.shard_map(
        shards,
        mesh=mesh,
        in_specs=(
            P(("dp", "seq"), None),
            P(("dp", "seq"), None),
            P(("dp", "seq"), None),
            P(("dp", "seq"), None),
            P(("dp", "seq"), None),
            P("dp", None),
            P(),
            P("dp", None),
            P(("dp", "seq")),
        ),
        out_specs=(
            P(("dp", "seq"), None),
            P(("dp", "seq"), None),
            P(("dp", "seq"), None),
            P(("dp", "seq"), None),
            P("dp", None),
        ),
        check_vma=False,
    )
```

profile of v0, /device:TPU:1, one launch (start us, length us, event | category | flops | bytes accessed | tf_op | source)
XLA Modules:
  0.0 1043.6 jit_solution(14746765452230040651)
XLA Ops:
  15.1 14.4 %all-gather.1 = s32[8,1,128]{2,1,0:T(1,128)S(1)} all-gather(s32[1,1,128]{2,1,0:T(1,128)S(1)} %fusion.97), channel_id=1, replica_groups=mesh['dp'=64,'seq'=8] {'seq'}, dimensions={0}, use_global_device_ids=true | all-gather | bytes 4608 | tf_op jit(solution)/shard_map/all_gather | solution.py:227
  30.2 5.0 reshape.214
  35.2 3.8 reshape.215
  40.5 6.1 reshape.216
  46.5 5.3 reshape.217
  51.9 10.1 all-gather
  64.3 25.7 %all-gather.11.cloned.1.call-done = bf16[1024,1024]{0,1:T(8,128)(2,1)} async-done(((bf16[128,1024]{0,1:T(8,128)(2,1)}), bf16[1024,1024]{0,1:T(8,128)(2,1)}) %all-gather.11.cloned.1.call-update) | async-done | bytes 2097168 | tf_op jit(solution)/shard_map/all_gather | solution.py:127
  90.1 14.6 %while.44 = (s32[]{:T(128)}, f32[128,1024]{0,1:T(8,128)S(1)}, s32[128]{0:T(128)S(1)}, s32[1024]{0:T(1024)S(1)}, s32[1024]{0:T(1024)S(1)}, /*index=5*/bf16[1024,1...) while((s32[]{:T(128)}, f32[128,1024]{0,1:T(8,128)S(1)}, ...), condition=%wide.region_7.8_spmd.clone, body=%wide.region_3.7_spmd.clone.sunk | while | flops 271188096 | bytes 8859939 | solution.py:167
  92.6 3.5 conditional.9
  105.2 121.2 %all-gather.13.cloned.1.call-done = bf16[1024,1024]{1,0:T(8,128)(2,1)} async-done(((bf16[16,1024]{1,0:T(8,128)(2,1)}), bf16[1024,1024]{1,0:T(8,128)(2,1)}) %all-gather.13.cloned.1.call-update) | async-done | bytes 2097168 | tf_op jit(solution)/shard_map/all_gather | solution.py:183
  226.4 2.8 fusion.89
  231.2 5.2 convolution_bitcast_fusion.6
  236.4 5.4 copy.118
  244.7 2.0 copy.107
  246.8 20.0 %all-gather.2 = s32[8,1,128]{2,1,0:T(1,128)S(1)} all-gather(s32[1,1,128]{2,1,0:T(1,128)S(1)} %fusion.116), channel_id=1, replica_groups=mesh['dp'=64,'seq'=8] {'seq'}, dimensions={0}, use_global_device_ids=true | all-gather | bytes 4608 | tf_op jit(solution)/shard_map/all_gather | solution.py:228
  266.8 14.2 %while.45 = (s32[]{:T(128)}, f32[128,1024]{0,1:T(8,128)S(1)}, s32[128]{0:T(128)S(1)}, s32[1024]{0:T(1024)S(1)}, s32[1024]{0:T(1024)S(1)}, /*index=5*/bf16[1024,1...) while((s32[]{:T(128)}, f32[128,1024]{0,1:T(8,128)S(1)}, ...), condition=%wide.region_16.17_spmd.clone, body=%wide.region_12.16_spmd.clone.sunk | while | flops 339345536 | bytes 11743031 | solution.py:167
  268.7 5.8 conditional.10
  268.7 2.1 constant_dynamic-slice_fusion.2
  272.6 1.9 fusion.31
  281.9 4.0 copy.106
  285.9 20.4 %all-gather.17.cloned.1.call-done = bf16[1024,1024]{0,1:T(8,128)(2,1)} async-done(((bf16[128,1024]{0,1:T(8,128)(2,1)}), bf16[1024,1024]{0,1:T(8,128)(2,1)}) %all-gather.17.cloned.1.call-update) | async-done | bytes 2097168 | tf_op jit(solution)/shard_map/all_gather | solution.py:225
  306.3 27.9 %while.46 = (s32[]{:T(128)}, f32[128,1024]{0,1:T(8,128)S(1)}, f32[128,1024]{0,1:T(8,128)}, s32[1024]{0:T(1024)S(1)}, s32[128]{0:T(128)S(1)}, /*index=5*/s32[1024...) while((s32[]{:T(128)}, f32[128,1024]{0,1:T(8,128)S(1)}, ...), condition=%wide.region_22.23_spmd.clone, body=%wide.region_18.22_spmd.clone.sunk | while | flops 408289408 | bytes 17543012 | solution.py:254
  308.1 6.3 conditional.11
  308.1 2.1 constant_dynamic-slice_fusion.4
  310.9 1.9 fusion.57
  317.4 6.3 conditional.11
  317.4 2.2 constant_dynamic-slice_fusion.4
  323.7 2.2 select_add_fusion.9
  327.8 2.2 select_add_fusion.9
  332.0 2.2 select_add_fusion.9
  336.9 663.5 %reduce-scatter.4.cloned.1.call-done = f32[16,1024]{1,0:T(8,128)} async-done(((f32[1024,1024]{1,0:T(8,128)}), f32[16,1024]{1,0:T(8,128)}) %reduce-scatter.4.cloned.1.call-update) | async-done | bytes 65552
  1001.4 34.6 %psum.7 = bf16[16,1024]{0,1:T(8,128)(2,1)S(1)} all-reduce(bf16[16,1024]{0,1:T(8,128)(2,1)S(1)} %copy.119), channel_id=1, replica_groups=mesh['dp'=64,'seq'=8] {'seq'}, use_global_device_ids=true, to_apply=%region_24.25 | all-reduce | flops 16384 | bytes 65536 | tf_op jit(solution)/shard_map/psum | solution.py:202
  (178 shorter events, 54.8 us)
Async XLA Ops:
  7.2 219.2 %copy-start = (f32[128,1024]{1,0:T(8,128)S(1)}, f32[128,1024]{1,0:T(8,128)}, u32[]{:S(2)}) copy-start(f32[128,1024]{1,0:T(8,128)} %param.25) | copy-start | bytes 1572868
  7.2 57.1 %all-gather.9.cloned.1.call-start = ((), (), s32[]{:S(2)}) async-start(), calls=%async_computation.1 | async-start | bytes 2359296 | tf_op jit(solution)/shard_map/all_gather | solution.py:128
  9.1 81.0 %all-gather.11.cloned.1.call-start = ((), (), s32[]{:S(2)}) async-start(), calls=%async_computation.2 | async-start | bytes 2359296 | tf_op jit(solution)/shard_map/all_gather | solution.py:127
  11.0 215.4 %all-gather.13.cloned.1.call-start = ((), (), s32[]{:S(2)}) async-start(), calls=%async_computation.3 | async-start | bytes 2129920 | tf_op jit(solution)/shard_map/all_gather | solution.py:183
  12.5 269.4 %all-gather.15.cloned.1.call-start = ((), (), s32[]{:S(2)}) async-start(), calls=%async_computation.4 | async-start | bytes 2359296 | tf_op jit(solution)/shard_map/all_gather | solution.py:226
  46.5 5.3 copy-start.8
  51.9 38.2 %copy-start.5 = (bf16[8,256,510]{2,1,0:T(8,128)(2,1)}, bf16[8,256,510]{2,1,0:T(8,128)(2,1)S(1)}, u32[]{:S(2)}) copy-start(bf16[8,256,510]{2,1,0:T(8,128)(2,1)S(1)} %reshape.217) | copy-start | bytes 6266884
  51.9 38.2 %copy-start.1 = (bf16[128,1024]{1,0:T(8,128)(2,1)S(1)}, bf16[128,1024]{1,0:T(8,128)(2,1)}, u32[]{:S(2)}) copy-start(bf16[128,1024]{1,0:T(8,128)(2,1)} %param.21) | copy-start | bytes 786436
  104.7 121.7 %copy-start.7 = (bf16[128,1024]{1,0:T(8,128)(2,1)S(1)}, bf16[128,1024]{1,0:T(8,128)(2,1)}, u32[]{:S(2)}) copy-start(bf16[128,1024]{1,0:T(8,128)(2,1)} %param.24) | copy-start | bytes 786436
  230.2 76.1 %all-gather.17.cloned.1.call-start = ((), (), s32[]{:S(2)}) async-start(), calls=%async_computation.5 | async-start | bytes 2359296 | tf_op jit(solution)/shard_map/all_gather | solution.py:225
  231.1 769.2 %reduce-scatter.4.cloned.1.call-start = ((), (), s32[]{:S(2)}) async-start(), calls=%async_computation.6 | async-start | bytes 4259840
  241.8 1.6 copy-start.6
  281.9 24.4 %copy-start.2 = (f32[128,1024]{0,1:T(8,128)S(1)}, f32[128,1024]{0,1:T(8,128)}, u32[]{:S(2)}) copy-start(f32[128,1024]{0,1:T(8,128)} %custom-call.2) | copy-start | bytes 1572868
  281.9 24.4 %copy-start.4 = (bf16[128,1024]{1,0:T(8,128)(2,1)S(1)}, bf16[128,1024]{1,0:T(8,128)(2,1)}, u32[]{:S(2)}) copy-start(bf16[128,1024]{1,0:T(8,128)(2,1)} %param.22) | copy-start | bytes 786436
  308.1 2.5 copy-start.3
  317.4 2.5 copy-start.3
Sparse Core Ops, SparseCore 0:
  10.7 40.6 all-gather.8
  54.0 35.9 all-gather.10
  93.6 132.7 all-gather.12
  230.3 38.0 all-gather.14
  271.0 35.2 all-gather.16
  310.6 689.7 reduce-scatter.3
where the time goes:
time: 1050 us; the launch traced here: 1040 us
  waiting for transfers between devices  831 us (79%)
  blocking collectives  79.1 us (8%)
  local copies, waits for them, and re-layouts  57.7 us (5%)
  other arithmetic  28.1 us (3%)
  matrix products  24.5 us (2%)
  between operations  14.3 us (1%)
    unnamed x7, waiting for transfers between devices  664 us
    all_gather x1, waiting for transfers between devices, shards(): lax.all_gather(out_weight.astype(jnp.bfloat16), 'dp', axis=0, tiled=True)  121 us
    unnamed x32, local copies, waits for them, and re-layouts  41.3 us
    psum x1, blocking collectives, shards(): lax.psum(share.astype(jnp.bfloat16), 'seq').astype(jnp.float32)  34.6 us
    all_gather x1, waiting for transfers between devices, shards(): lax.all_gather(key_vectors, 'seq', axis=0, tiled=True)  25.7 us
  transfers between devices with their start and end apart: 6, of which 4 were waited for; matrix products, arithmetic and copies ran while one was open for 10% of the time, Pallas kernels for 0%

commit v1 on v0

v1 whole, which is shorter than its diff:
```python
import functools

import jax
import jax.numpy as jnp
from jax import lax
from jax.experimental import pallas as pl
from jax.experimental.pallas import tpu as pltpu
from jax.sharding import PartitionSpec as P

norm_eps = 1e-06
MESH = pl.DeviceIdType.MESH
F32 = jnp.float32
BF16 = jnp.bfloat16
T = 128
N = 8
NY = 4
NZ = 16
BAND = 4
NT = (((1,), (1,)), ((), ()))


def rows(i):
    return pl.ds(i * T, T)


def dyn(i):
    return pl.ds(pl.multiple_of(i * T, T), T)


def kernel(
    q_in, k_in, v_in, g_in, og_in, w_in, tb_in, len_in, st_in,
    dq_out, dk_out, dv_out, dg_out, wg_out,
    q, k, v, g, og, w, stamps, stats,
    kt, vt, gt, ngt, ggt, at, dat, gated, probs, slope, ds,
    dq, dk, dv, dg, wg, ry, zs, rz, fin,
    in_send, in_recv, w_send, w_recv, out_send, out_recv, own_sem,
):
    dp, me = lax.axis_index("dp"), lax.axis_index("seq")
    z, y = lax.div(dp, NY), lax.rem(dp, NY)

    def seq_peer(s):
        return (dp, s)

    def z_peer(zz):
        return (zz * NY + y, me)

    def y_peer(yy):
        return (z * NY + yy, me)

    def send(src, dst, ssem, rsem, device):
        pltpu.make_async_remote_copy(
            src_ref=src, dst_ref=dst, send_sem=ssem, recv_sem=rsem, device_id=device, device_id_type=MESH
        ).start()

    def wait(ref, sem):
        pltpu.make_async_copy(ref, ref, sem).wait()

    barrier = pltpu.get_barrier_semaphore()
    for d in range(1, N):
        pl.semaphore_signal(barrier, inc=1, device_id=seq_peer(lax.rem(me + d, N)), device_id_type=MESH)
    for d in range(1, NY):
        pl.semaphore_signal(barrier, inc=1, device_id=y_peer(lax.rem(y + d, NY)), device_id_type=MESH)
    for d in range(1, NZ):
        pl.semaphore_signal(barrier, inc=1, device_id=z_peer(lax.rem(z + d, NZ)), device_id_type=MESH)

    og[dyn(me), :] = og_in[...].astype(BF16)
    w[z, y] = w_in[:, dyn(me)].astype(BF16)
    stamps[me] = jnp.broadcast_to(st_in[...], (8, T))
    heads_of = tb_in[...].astype(F32)
    mine = jnp.where(lax.broadcasted_iota(jnp.int32, heads_of.shape, 1) == me, heads_of, 0.0)
    column = jnp.sum(mine, axis=1, keepdims=True)
    table = jnp.transpose(jnp.broadcast_to(column, (T, T)))

    pl.semaphore_wait(barrier, N - 1 + NY - 1 + NZ - 1)

    for d in range(1, N):
        peer = lax.rem(me + d, N)
        send(stamps.at[me], stamps.at[me], in_send.at[0], in_recv.at[0], seq_peer(peer))
    for n, (src, dst) in enumerate(((q_in, q), (k_in, k), (v_in, v))):
        pltpu.make_async_copy(src.at[:, dyn(me)], dst.at[dyn(me), :], in_recv.at[1 + n]).start()
        for d in range(1, N):
            peer = lax.rem(me + d, N)
            send(src.at[:, dyn(peer)], dst.at[dyn(me), :], in_send.at[1 + n], in_recv.at[1 + n], seq_peer(peer))
    for d in range(1, NZ):
        send(w.at[z, y], w.at[z, y], w_send.at[0], w_recv.at[0], z_peer(lax.rem(z + d, NZ)))
    for d in range(1, N):
        peer = lax.rem(me + d, N)
        send(og.at[dyn(me), :], og.at[dyn(me), :], in_send.at[5], in_recv.at[5], seq_peer(peer))
    pltpu.make_async_copy(g_in.at[:, dyn(me)], g.at[dyn(me), :], in_recv.at[4]).start()
    for d in range(1, N):
        peer = lax.rem(me + d, N)
        send(g_in.at[:, dyn(peer)], g.at[dyn(me), :], in_send.at[4], in_recv.at[4], seq_peer(peer))

    place = lax.broadcasted_iota(jnp.int32, (1, N * T), 1)
    end = jnp.int32(0)
    start = jnp.zeros((1, N * T), jnp.int32)
    for n in range(len_in.shape[1]):
        end = end + len_in[0, n]
        start = jnp.where(place >= end, end, start)
    below = lax.broadcasted_iota(jnp.int32, (T, T), 0)
    across = lax.broadcasted_iota(jnp.int32, (T, T), 1)

    wait(stamps.at[pl.ds(0, N - 1)], in_recv.at[0])
    wait(q, in_recv.at[1])
    wait(k, in_recv.at[2])
    for i in range(N):
        query_stamps = stamps[i, 0:1, :]
        for j in range(max(0, i - BAND), i + 1):
            key_stamps = jnp.transpose(jnp.broadcast_to(stamps[j, 0:1, :], (T, T)))
            bucket = jnp.clip(query_stamps - key_stamps, 0, T - 1)
            bias = jnp.take_along_axis(table, bucket, axis=1)
            score = lax.dot_general(k[rows(j), :], q[rows(i), :], NT, preferred_element_type=F32) + bias
            allowed = below >= start[:, i * T : (i + 1) * T] - j * T
            if i == j:
                allowed = allowed & (below <= across)
            sigma = jnp.where(allowed, 0.5 * jnp.tanh(0.5 * score) + 0.5, 0.0)
            prob = score * sigma
            probs[rows(j), rows(i)] = prob.astype(BF16)
            slope[rows(j), rows(i)] = sigma + prob * (1.0 - sigma)

    wait(w.at[pl.ds(0, NZ - 1), 0], w_recv.at[0])
    for d in range(1, NY):
        send(w.at[:, y], w.at[:, y], w_send.at[1], w_recv.at[1], y_peer(lax.rem(y + d, NY)))

    wait(v, in_recv.at[3])
    for i in range(N):
        vt[:, rows(i)] = jnp.transpose(v[rows(i), :])
        kt[:, rows(i)] = jnp.transpose(k[rows(i), :])
    for i in range(N):
        lo = max(0, i - BAND) * T
        hi = (i + 1) * T
        at[:, rows(i)] = jnp.dot(vt[:, lo:hi], probs[lo:hi, rows(i)], preferred_element_type=F32)

    wait(w.at[:, pl.ds(0, NY - 1)], w_recv.at[1])
    wait(og.at[pl.ds(0, (N - 1) * T), :], in_recv.at[5])
    wait(g, in_recv.at[4])
    weight = w[...].reshape(N * T, T)
    for i in range(N):
        gated_grad = jnp.transpose(jnp.dot(og[rows(i), :], weight, preferred_element_type=F32))
        gate = jnp.transpose(g[rows(i), :].astype(F32))
        normed_grad = gated_grad * gate
        attended = at[:, rows(i)]
        mean = jnp.sum(attended, axis=0, keepdims=True) * (1.0 / T)
        centred = attended - mean
        spread = jnp.sum(centred * centred, axis=0, keepdims=True)
        grad_sum = jnp.sum(normed_grad, axis=0, keepdims=True)
        cross = jnp.sum(normed_grad * centred, axis=0, keepdims=True)
        gt[:, rows(i)] = gate
        ggt[:, rows(i)] = gated_grad
        ngt[:, rows(i)] = normed_grad
        for n, value in enumerate((mean, spread, grad_sum, cross)):
            stats[me, 2 * n + i // 4 : 2 * n + i // 4 + 1, (i % 4) * T : (i % 4 + 1) * T] = value
    for d in range(1, N):
        send(stats.at[me], stats.at[me], in_send.at[6], in_recv.at[6], seq_peer(lax.rem(me + d, N)))
    wait(stats.at[pl.ds(0, N - 1)], in_recv.at[6])

    width = N * T
    for i in range(N):
        def stat(n):
            return stats[:, 2 * n + i // 4, (i % 4) * T : (i % 4 + 1) * T]

        means, grad_sums = stat(0), stat(2)
        mean = jnp.sum(means, axis=0, keepdims=True) * (1.0 / N)
        apart = means - mean
        spread = jnp.sum(stat(1), axis=0, keepdims=True) + T * jnp.sum(apart * apart, axis=0, keepdims=True)
        inverse = lax.rsqrt(spread * (1.0 / width) + norm_eps)
        grad_mean = jnp.sum(grad_sums, axis=0, keepdims=True) * (1.0 / width)
        cross = jnp.sum(stat(3) + apart * grad_sums, axis=0, keepdims=True) * inverse * (1.0 / width)
        normed = (at[:, rows(i)] - mean) * inverse
        gated[:, rows(i)] = (normed * gt[:, rows(i)]).astype(BF16)
        dat[:, rows(i)] = (inverse * (ngt[:, rows(i)] - grad_mean - normed * cross)).astype(BF16)
        dg[rows(i), :] = jnp.transpose(ggt[:, rows(i)] * normed).astype(BF16)

    def deliver(n, src, dst):
        pltpu.make_async_copy(src.at[dyn(me), :], dst.at[:, dyn(me)], out_recv.at[n]).start()
        for d in range(1, N):
            peer = lax.rem(me + d, N)
            send(src.at[dyn(peer), :], dst.at[:, dyn(me)], out_send.at[n], out_recv.at[n], seq_peer(peer))

    deliver(0, dg, dg_out)

    terms = jnp.dot(gated[...], og[...], preferred_element_type=F32)
    per = T // (NY * 16)
    for i in range(N):
        block = jnp.transpose(terms[:, i * T : (i + 1) * T]).astype(BF16)
        wg[i * per : (i + 1) * per] = block.reshape(per, NY, 16, T)
    ry[y] = wg[:, y]
    for d in range(1, NY):
        yy = lax.rem(y + d, NY)
        send(wg.at[:, yy], ry.at[y], w_send.at[2], w_recv.at[2], y_peer(yy))

    for j in range(N):
        lo, hi = j * T, min(j + BAND + 1, N) * T
        dv[rows(j), :] = lax.dot_general(
            probs[rows(j), lo:hi], dat[:, lo:hi], NT, preferred_element_type=F32
        ).astype(BF16)
    deliver(1, dv, dv_out)
    for i in range(N):
        lo, hi = max(0, i - BAND) * T, (i + 1) * T
        for j in range(max(0, i - BAND), i + 1):
            prob_grad = jnp.dot(v[rows(j), :], dat[:, rows(i)], preferred_element_type=F32)
            ds[rows(j), rows(i)] = (prob_grad * slope[rows(j), rows(i)]).astype(BF16)

    wait(ry.at[pl.ds(0, NY - 1)], w_recv.at[2])
    total = ry[0].astype(F32)
    for n in range(1, NY):
        total = total + ry[n].astype(F32)
    zs[...] = total.astype(BF16)
    rz[z] = zs[z]
    for d in range(1, NZ):
        zz = lax.rem(z + d, NZ)
        send(zs.at[zz], rz.at[z], w_send.at[3], w_recv.at[3], z_peer(zz))

    for i in range(N):
        lo, hi = max(0, i - BAND) * T, (i + 1) * T
        dq[rows(i), :] = jnp.transpose(
            jnp.dot(kt[:, lo:hi], ds[lo:hi, rows(i)], preferred_element_type=F32)
        ).astype(BF16)
    deliver(2, dq, dq_out)
    for j in range(N):
        lo, hi = j * T, min(j + BAND + 1, N) * T
        dk[rows(j), :] = jnp.dot(ds[rows(j), lo:hi], q[lo:hi, :], preferred_element_type=F32).astype(BF16)
    deliver(3, dk, dk_out)

    wait(rz.at[pl.ds(0, NZ - 1)], w_recv.at[3])
    total = rz[0].astype(F32)
    for n in range(1, NZ):
        total = total + rz[n].astype(F32)
    fin[...] = total * (1.0 / T)
    pltpu.make_async_copy(fin, wg_out.at[:, dyn(me)], own_sem).start()
    for d in range(1, N):
        send(fin, wg_out.at[:, dyn(me)], out_send.at[4], out_recv.at[4], seq_peer(lax.rem(me + d, N)))

    wait(stamps.at[pl.ds(0, N - 1)], in_send.at[0])
    for n in range(1, 5):
        wait(q.at[pl.ds(0, (N - 1) * T), :], in_send.at[n])
    wait(og.at[pl.ds(0, (N - 1) * T), :], in_send.at[5])
    wait(stats.at[pl.ds(0, N - 1)], in_send.at[6])
    wait(w.at[pl.ds(0, NZ - 1), 0], w_send.at[0])
    wait(w.at[:, pl.ds(0, NY - 1)], w_send.at[1])
    wait(ry.at[pl.ds(0, NY - 1)], w_send.at[2])
    wait(rz.at[pl.ds(0, NZ - 1)], w_send.at[3])
    for n, dst in enumerate((dg_out, dv_out, dq_out, dk_out)):
        wait(dst, out_recv.at[n])
        wait(q.at[pl.ds(0, (N - 1) * T), :], out_send.at[n])
    wait(fin, own_sem)
    wait(wg_out.at[:, pl.ds(0, (N - 1) * T)], out_recv.at[4])
    wait(wg_out.at[:, pl.ds(0, (N - 1) * T)], out_send.at[4])


def shards(queries, keys, values, gates, out_grad, out_weight, time_bias, lengths, stamps):
    width = N * T
    event = jax.ShapeDtypeStruct((T, width), BF16)
    block = pltpu.VMEM((width, T), BF16)
    across16 = pltpu.VMEM((T, width), BF16)
    across32 = pltpu.VMEM((T, width), F32)
    hbm = pl.BlockSpec(memory_space=pl.ANY)
    vmem = pl.BlockSpec(memory_space=pltpu.VMEM)
    smem = pl.BlockSpec(memory_space=pltpu.SMEM)
    return pl.pallas_call(
        kernel,
        out_shape=(event, event, event, event, jax.ShapeDtypeStruct((16, width), F32)),
        in_specs=[hbm, hbm, hbm, hbm, vmem, vmem, vmem, smem, vmem],
        out_specs=(hbm,) * 5,
        scratch_shapes=[
            block, block, block, block,
            pltpu.VMEM((width, width), BF16),
            pltpu.VMEM((NZ, NY, 16, T), BF16),
            pltpu.VMEM((N, 8, T), jnp.int32),
            pltpu.VMEM((N, 8, 4 * T), F32),
            across16, across16,
            across32, across32, across32, across32,
            across16, across16,
            pltpu.VMEM((width, width), BF16),
            pltpu.VMEM((width, width), F32),
            pltpu.VMEM((width, width), BF16),
            block, block, block, block,
            pltpu.VMEM((NZ, NY, 16, T), BF16),
            pltpu.VMEM((NY, NZ, 16, T), BF16),
            pltpu.VMEM((NZ, 16, T), BF16),
            pltpu.VMEM((NZ, 16, T), BF16),
            pltpu.VMEM((16, T), F32),
            pltpu.SemaphoreType.DMA((7,)),
            pltpu.SemaphoreType.DMA((7,)),
            pltpu.SemaphoreType.DMA((4,)),
            pltpu.SemaphoreType.DMA((4,)),
            pltpu.SemaphoreType.DMA((5,)),
            pltpu.SemaphoreType.DMA((5,)),
            pltpu.SemaphoreType.DMA,
        ],
        compiler_params=pltpu.CompilerParams(
            collective_id=0, has_side_effects=True, vmem_limit_bytes=48 * 1024 * 1024
        ),
    )(queries, keys, values, gates, out_grad, out_weight, time_bias, lengths, stamps.reshape(1, T))


def solution(mesh):
    events = P(("dp", "seq"), None)
    return jax.shard_map(
        shards,
        mesh=mesh,
        in_specs=(
            events, events, events, events, events, P("dp", None), P(), P("dp", None), P(("dp", "seq")),
        ),
        out_specs=(events, events, events, events, P("dp", None)),
        check_vma=False,
    )
```

time: 1050 us -> 87.4 us (0.08)
  waiting for transfers between devices: 831 us -> 0 us
  blocking collectives: 79.1 us -> 0 us
  Pallas kernels: 0 us -> 76.4 us
  local copies, waits for them, and re-layouts: 57.7 us -> 9.93 us
  other arithmetic: 28.1 us -> 0 us
  matrix products: 24.5 us -> 0 us
  between operations: 14.3 us -> 0.68 us
    unnamed x7 -> x0, waiting for transfers between devices: 664 us -> none
    all_gather x5 -> x0, waiting for transfers between devices: 167 us -> none  [the longest x1 121 us: shards(): lax.all_gather(out_weight.astype(jnp.bfloat16), 'dp', axis=0, tiled=True)]
    pallas_call x0 -> x1, Pallas kernels: none -> 76.4 us  [shards(): pl.pallas_call(kernel, out_shape=(event, event, event, event, jax.ShapeDt...]
    all_gather x3 -> x0, blocking collectives: 44.5 us -> none  [the longest x1 20 us: shards(): piece_stamps = lax.all_gather(query_stamps, 'seq', axis=0, tiled=True)]
    psum x1 -> x0, blocking collectives: 34.6 us -> none  [shards(): lax.psum(share.astype(jnp.bfloat16), 'seq').astype(jnp.float32)]
    unnamed x32 -> x22, local copies, waits for them, and re-layouts: 41.3 us -> 9.93 us
    dot_general x17 -> x0, matrix products: 24.5 us -> none  [the longest x1 5.24 us: shards(): lax.dot_general(columns, gated, (((0,), (0,)), ((), ())), precision=exact...]
  transfers between devices with their start and end apart: 6 -> 0, of which waited for: 4 -> 0; matrix products, arithmetic and copies ran while one was open for 10% -> 0% of each run, Pallas kernels for 0% -> 0%
where the time goes in v1:
time: 87.4 us; the launch traced here: 87 us
  Pallas kernels  76.4 us (87%)
  local copies, waits for them, and re-layouts  9.93 us (11%)
    pallas_call x1, Pallas kernels, shards(): pl.pallas_call(kernel, out_shape=(event, event, event, event, jax.ShapeDt...  76.4 us
    unnamed x22, local copies, waits for them, and re-layouts  9.93 us

profile of v1, /device:TPU:1, one launch (start us, length us, event | category | flops | bytes accessed | tf_op | source)
XLA Modules:
  0.0 87.0 jit_solution(2699470842667193379)
XLA Ops:
  0.6 0.0 copy-start.6
  0.6 0.0 copy-start.7
  0.7 0.8 copy.14.tb_in
  1.5 0.0 copy-done.6
  1.5 0.0 copy-done.7
  1.5 0.0 copy-start
  1.5 1.0 %copy-done = f32[128,1024]{1,0:T(8,128)S(1)} copy-done((f32[128,1024]{1,0:T(8,128)S(1)}, f32[128,1024]{1,0:T(8,128)}, u32[]{:S(2)}) %copy-start) | copy-done | bytes 524312
  2.5 0.0 copy-start.1
  2.5 0.9 %copy-done.1 = bf16[128,1024]{1,0:T(8,128)(2,1)S(1)} copy-done((bf16[128,1024]{1,0:T(8,128)(2,1)S(1)}, bf16[128,1024]{1,0:T(8,128)(2,1)}, u32[]{:S(2)}) %copy-start.1) | copy-done | bytes 262168
  3.5 0.0 copy-start.2
  3.5 0.9 %copy-done.2 = bf16[128,1024]{1,0:T(8,128)(2,1)S(1)} copy-done((bf16[128,1024]{1,0:T(8,128)(2,1)S(1)}, bf16[128,1024]{1,0:T(8,128)(2,1)}, u32[]{:S(2)}) %copy-start.2) | copy-done | bytes 262168
  4.4 0.0 copy-start.3
  4.4 0.9 %copy-done.3 = bf16[128,1024]{1,0:T(8,128)(2,1)S(1)} copy-done((bf16[128,1024]{1,0:T(8,128)(2,1)S(1)}, bf16[128,1024]{1,0:T(8,128)(2,1)}, u32[]{:S(2)}) %copy-start.3) | copy-done | bytes 262168
  5.4 0.0 copy-start.4
  5.4 0.9 %copy-done.4 = bf16[128,1024]{1,0:T(8,128)(2,1)S(1)} copy-done((bf16[128,1024]{1,0:T(8,128)(2,1)S(1)}, bf16[128,1024]{1,0:T(8,128)(2,1)}, u32[]{:S(2)}) %copy-start.4) | copy-done | bytes 262168
  6.3 0.0 copy-start.5
  6.3 0.8 copy-done.5
  7.2 76.4 %shard_map.128 = (bf16[128,1024]{1,0:T(8,128)(2,1)S(1)}, bf16[128,1024]{1,0:T(8,128)(2,1)S(1)}, bf16[128,1024]{1,0:T(8,128)(2,1)S(1)}, bf16[128,1024]{1,0:T(8,128)(2,1)S(1)}, f32[16,1024]{1,0:T(8,128)S(1)}) custom-call(bf16[128,1024]{1,0:T(8,128)(2,1)S(1)} %copy-done.1, bf16[128,1024]{1,0:T(8,128)(2,1)S(1)} %copy-done.2, bf16[128,1024]{1,0:T(8,128)(2,1)S(1)} %copy-done.3, ...), custom_call_target="tpu_custom_call" | custom-call | tf_op jit(solution)/shard_map/pallas_call | solution.py:260
  83.6 0.7 copy.20
  84.3 0.7 copy.21
  85.0 0.7 copy.22
  85.7 0.7 copy.23
  86.4 0.6 copy.24
Async XLA Ops:
  0.6 0.8 copy-start.6
  0.6 0.8 copy-start.7
  1.5 1.0 %copy-start = (f32[128,1024]{1,0:T(8,128)S(1)}, f32[128,1024]{1,0:T(8,128)}, u32[]{:S(2)}) copy-start(f32[128,1024]{1,0:T(8,128)} %og_in.1) | copy-start | bytes 1572868
  2.5 0.9 %copy-start.1 = (bf16[128,1024]{1,0:T(8,128)(2,1)S(1)}, bf16[128,1024]{1,0:T(8,128)(2,1)}, u32[]{:S(2)}) copy-start(bf16[128,1024]{1,0:T(8,128)(2,1)} %q_in.1) | copy-start | bytes 786436
  3.5 0.9 %copy-start.2 = (bf16[128,1024]{1,0:T(8,128)(2,1)S(1)}, bf16[128,1024]{1,0:T(8,128)(2,1)}, u32[]{:S(2)}) copy-start(bf16[128,1024]{1,0:T(8,128)(2,1)} %k_in.1) | copy-start | bytes 786436
  4.4 0.9 %copy-start.3 = (bf16[128,1024]{1,0:T(8,128)(2,1)S(1)}, bf16[128,1024]{1,0:T(8,128)(2,1)}, u32[]{:S(2)}) copy-start(bf16[128,1024]{1,0:T(8,128)(2,1)} %v_in.1) | copy-start | bytes 786436
  5.4 0.9 %copy-start.4 = (bf16[128,1024]{1,0:T(8,128)(2,1)S(1)}, bf16[128,1024]{1,0:T(8,128)(2,1)}, u32[]{:S(2)}) copy-start(bf16[128,1024]{1,0:T(8,128)(2,1)} %g_in.1) | copy-start | bytes 786436
  6.3 0.8 copy-start.5

commit v2 on v1

--- a/solution.py
+++ b/solution.py
@@ -28,12 +28,13 @@
 
 
 def kernel(
-    q_in, k_in, v_in, g_in, og_in, w_in, tb_in, len_in, st_in,
+    q_in, k_in, v_in, g_in, og_hbm, w_hbm, tb_hbm, len_hbm, st_hbm,
     dq_out, dk_out, dv_out, dg_out, wg_out,
     q, k, v, g, og, w, stamps, stats,
     kt, vt, gt, ngt, ggt, at, dat, gated, probs, slope, ds,
     dq, dk, dv, dg, wg, ry, zs, rz, fin,
-    in_send, in_recv, w_send, w_recv, out_send, out_recv, own_sem,
+    og_in, w_in, tb_in, len_in, st_in,
+    in_send, in_recv, og_send, og_recv, w_send, w_recv, out_send, out_recv, own_sem, load_sem,
 ):
     dp, me = lax.axis_index("dp"), lax.axis_index("seq")
     z, y = lax.div(dp, NY), lax.rem(dp, NY)
@@ -46,14 +47,41 @@
 
     def y_peer(yy):
         return (z * NY + yy, me)
+
+    chip, core = lax.div(me, 2), lax.rem(me, 2)
+    left, right = lax.rem(me + N - 2, N), lax.rem(me + 2, N)
+    facing = lax.rem(me + 4, N)
+    sibling = 2 * chip + 1 - core
+
+    def half(owner, part):
+        return og.at[pl.ds(pl.multiple_of(owner * T + part * (T // 2), T // 2), T // 2), :]
+
+    def pass_on(n, owner, part, peer):
+        ref = half(owner, part)
+        send(ref, ref, og_send.at[n], og_recv.at[n], seq_peer(peer))
+        expect('og%d' % n, half(0, 0), og_recv.at[n])
+        expect('og%d sent' % n, half(0, 0), og_send.at[n])
 
     def send(src, dst, ssem, rsem, device):
         pltpu.make_async_remote_copy(
             src_ref=src, dst_ref=dst, send_sem=ssem, recv_sem=rsem, device_id=device, device_id_type=MESH
         ).start()
 
-    def wait(ref, sem):
+    expected = {}
+
+    def expect(name, ref, sem):
+        expected[name] = (ref, sem)
+
+    def wait(name):
+        ref, sem = expected.pop(name)
         pltpu.make_async_copy(ref, ref, sem).wait()
+
+    loads = [
+        pltpu.make_async_copy(src, dst, load_sem.at[n])
+        for n, (src, dst) in enumerate(((og_hbm, og_in), (w_hbm, w_in), (tb_hbm, tb_in), (len_hbm, len_in), (st_hbm, st_in)))
+    ]
+    for load in loads:
+        load.start()
 
     barrier = pltpu.get_barrier_semaphore()
     for d in range(1, N):
@@ -63,34 +91,46 @@
     for d in range(1, NZ):
         pl.semaphore_signal(barrier, inc=1, device_id=z_peer(lax.rem(z + d, NZ)), device_id_type=MESH)
 
+    for load in loads:
+        load.wait()
     og[dyn(me), :] = og_in[...].astype(BF16)
     w[z, y] = w_in[:, dyn(me)].astype(BF16)
     stamps[me] = jnp.broadcast_to(st_in[...], (8, T))
     heads_of = tb_in[...].astype(F32)
-    mine = jnp.where(lax.broadcasted_iota(jnp.int32, heads_of.shape, 1) == me, heads_of, 0.0)
-    column = jnp.sum(mine, axis=1, keepdims=True)
-    table = jnp.transpose(jnp.broadcast_to(column, (T, T)))
+    mine = jnp.where(lax.broadcasted_iota(jnp.int32, heads_of.shape, 0) == me, heads_of, 0.0)
+    table = jnp.broadcast_to(jnp.sum(mine, axis=0, keepdims=True), (T, T))
 
     pl.semaphore_wait(barrier, N - 1 + NY - 1 + NZ - 1)
 
     for d in range(1, N):
         peer = lax.rem(me + d, N)
         send(stamps.at[me], stamps.at[me], in_send.at[0], in_recv.at[0], seq_peer(peer))
+    expect('stamps', stamps.at[pl.ds(0, N - 1)], in_recv.at[0])
+    expect('stamps sent', stamps.at[pl.ds(0, N - 1)], in_send.at[0])
     for n, (src, dst) in enumerate(((q_in, q), (k_in, k), (v_in, v))):
         pltpu.make_async_copy(src.at[:, dyn(me)], dst.at[dyn(me), :], in_recv.at[1 + n]).start()
         for d in range(1, N):
             peer = lax.rem(me + d, N)
             send(src.at[:, dyn(peer)], dst.at[dyn(me), :], in_send.at[1 + n], in_recv.at[1 + n], seq_peer(peer))
+        expect('qkv'[n], dst, in_recv.at[1 + n])
+        expect('qkv'[n] + ' sent', q.at[pl.ds(0, (N - 1) * T), :], in_send.at[1 + n])
     for d in range(1, NZ):
         send(w.at[z, y], w.at[z, y], w_send.at[0], w_recv.at[0], z_peer(lax.rem(z + d, NZ)))
-    for d in range(1, N):
-        peer = lax.rem(me + d, N)
-        send(og.at[dyn(me), :], og.at[dyn(me), :], in_send.at[5], in_recv.at[5], seq_peer(peer))
+    expect('w z', w.at[pl.ds(0, NZ - 1), 0], w_recv.at[0])
+    expect('w z sent', w.at[pl.ds(0, NZ - 1), 0], w_send.at[0])
+    pass_on(0, me, 0, right)
+    pass_on(1, me, 1, left)
+    pass_on(2, me, 1, right)
+    pass_on(3, me, 0, left)
+    pass_on(6, me, 0, sibling)
+    pass_on(7, me, 1, sibling)
     pltpu.make_async_copy(g_in.at[:, dyn(me)], g.at[dyn(me), :], in_recv.at[4]).start()
     for d in range(1, N):
         peer = lax.rem(me + d, N)
         send(g_in.at[:, dyn(peer)], g.at[dyn(me), :], in_send.at[4], in_recv.at[4], seq_peer(peer))
 
+    expect('g', g, in_recv.at[4])
+    expect('g sent', q.at[pl.ds(0, (N - 1) * T), :], in_send.at[4])
     place = lax.broadcasted_iota(jnp.int32, (1, N * T), 1)
     end = jnp.int32(0)
     start = jnp.zeros((1, N * T), jnp.int32)
@@ -100,9 +140,9 @@
     below = lax.broadcasted_iota(jnp.int32, (T, T), 0)
     across = lax.broadcasted_iota(jnp.int32, (T, T), 1)
 
-    wait(stamps.at[pl.ds(0, N - 1)], in_recv.at[0])
-    wait(q, in_recv.at[1])
-    wait(k, in_recv.at[2])
+    wait('stamps')
+    wait('q')
+    wait('k')
     for i in range(N):
         query_stamps = stamps[i, 0:1, :]
         for j in range(max(0, i - BAND), i + 1):
@@ -118,11 +158,23 @@
             probs[rows(j), rows(i)] = prob.astype(BF16)
             slope[rows(j), rows(i)] = sigma + prob * (1.0 - sigma)
 
-    wait(w.at[pl.ds(0, NZ - 1), 0], w_recv.at[0])
+    wait('og0')
+    pass_on(4, left, 0, right)
+    wait('og1')
+    pass_on(5, right, 1, left)
+    pass_on(8, left, 0, sibling)
+    pass_on(9, right, 1, sibling)
+    wait('og2')
+    pass_on(10, left, 1, sibling)
+    wait('og3')
+    pass_on(11, right, 0, sibling)
+    wait('w z')
     for d in range(1, NY):
         send(w.at[:, y], w.at[:, y], w_send.at[1], w_recv.at[1], y_peer(lax.rem(y + d, NY)))
-
-    wait(v, in_recv.at[3])
+    expect('w y', w.at[:, pl.ds(0, NY - 1)], w_recv.at[1])
+    expect('w y sent', w.at[:, pl.ds(0, NY - 1)], w_send.at[1])
+
+    wait('v')
     for i in range(N):
         vt[:, rows(i)] = jnp.transpose(v[rows(i), :])
         kt[:, rows(i)] = jnp.transpose(k[rows(i), :])
@@ -131,9 +183,14 @@
         hi = (i + 1) * T
         at[:, rows(i)] = jnp.dot(vt[:, lo:hi], probs[lo:hi, rows(i)], preferred_element_type=F32)
 
-    wait(w.at[:, pl.ds(0, NY - 1)], w_recv.at[1])
-    wait(og.at[pl.ds(0, (N - 1) * T), :], in_recv.at[5])
-    wait(g, in_recv.at[4])
+    wait('w y')
+    wait('og4')
+    pass_on(12, facing, 0, sibling)
+    wait('og5')
+    pass_on(13, facing, 1, sibling)
+    for n in range(6, 14):
+        wait('og%d' % n)
+    wait('g')
     weight = w[...].reshape(N * T, T)
     for i in range(N):
         gated_grad = jnp.transpose(jnp.dot(og[rows(i), :], weight, preferred_element_type=F32))
@@ -152,7 +209,9 @@
             stats[me, 2 * n + i // 4 : 2 * n + i // 4 + 1, (i % 4) * T : (i % 4 + 1) * T] = value
     for d in range(1, N):
         send(stats.at[me], stats.at[me], in_send.at[6], in_recv.at[6], seq_peer(lax.rem(me + d, N)))
-    wait(stats.at[pl.ds(0, N - 1)], in_recv.at[6])
+    expect('stats', stats.at[pl.ds(0, N - 1)], in_recv.at[6])
+    expect('stats sent', stats.at[pl.ds(0, N - 1)], in_send.at[6])
+    wait('stats')
 
     width = N * T
     for i in range(N):
@@ -176,6 +235,8 @@
         for d in range(1, N):
             peer = lax.rem(me + d, N)
             send(src.at[dyn(peer), :], dst.at[:, dyn(me)], out_send.at[n], out_recv.at[n], seq_peer(peer))
+        expect('out%d' % n, dst, out_recv.at[n])
+        expect('out%d sent' % n, q.at[pl.ds(0, (N - 1) * T), :], out_send.at[n])
 
     deliver(0, dg, dg_out)
 
@@ -188,6 +249,8 @@
     for d in range(1, NY):
         yy = lax.rem(y + d, NY)
         send(wg.at[:, yy], ry.at[y], w_send.at[2], w_recv.at[2], y_peer(yy))
+    expect('ry', ry.at[pl.ds(0, NY - 1)], w_recv.at[2])
+    expect('ry sent', ry.at[pl.ds(0, NY - 1)], w_send.at[2])
 
     for j in range(N):
         lo, hi = j * T, min(j + BAND + 1, N) * T
@@ -201,7 +264,7 @@
             prob_grad = jnp.dot(v[rows(j), :], dat[:, rows(i)], preferred_element_type=F32)
             ds[rows(j), rows(i)] = (prob_grad * slope[rows(j), rows(i)]).astype(BF16)
 
-    wait(ry.at[pl.ds(0, NY - 1)], w_recv.at[2])
+    wait('ry')
     total = ry[0].astype(F32)
     for n in range(1, NY):
         total = total + ry[n].astype(F32)
@@ -210,6 +273,8 @@
     for d in range(1, NZ):
         zz = lax.rem(z + d, NZ)
         send(zs.at[zz], rz.at[z], w_send.at[3], w_recv.at[3], z_peer(zz))
+    expect('rz', rz.at[pl.ds(0, NZ - 1)], w_recv.at[3])
+    expect('rz sent', rz.at[pl.ds(0, NZ - 1)], w_send.at[3])
 
     for i in range(N):
         lo, hi = max(0, i - BAND) * T, (i + 1) * T
@@ -222,7 +287,7 @@
         dk[rows(j), :] = jnp.dot(ds[rows(j), lo:hi], q[lo:hi, :], preferred_element_type=F32).astype(BF16)
     deliver(3, dk, dk_out)
 
-    wait(rz.at[pl.ds(0, NZ - 1)], w_recv.at[3])
+    wait('rz')
     total = rz[0].astype(F32)
     for n in range(1, NZ):
         total = total + rz[n].astype(F32)
@@ -231,36 +296,36 @@
     for d in range(1, N):
         send(fin, wg_out.at[:, dyn(me)], out_send.at[4], out_recv.at[4], seq_peer(lax.rem(me + d, N)))
 
-    wait(stamps.at[pl.ds(0, N - 1)], in_send.at[0])
-    for n in range(1, 5):
-        wait(q.at[pl.ds(0, (N - 1) * T), :], in_send.at[n])
-    wait(og.at[pl.ds(0, (N - 1) * T), :], in_send.at[5])
-    wait(stats.at[pl.ds(0, N - 1)], in_send.at[6])
-    wait(w.at[pl.ds(0, NZ - 1), 0], w_send.at[0])
-    wait(w.at[:, pl.ds(0, NY - 1)], w_send.at[1])
-    wait(ry.at[pl.ds(0, NY - 1)], w_send.at[2])
-    wait(rz.at[pl.ds(0, NZ - 1)], w_send.at[3])
-    for n, dst in enumerate((dg_out, dv_out, dq_out, dk_out)):
-        wait(dst, out_recv.at[n])
-        wait(q.at[pl.ds(0, (N - 1) * T), :], out_send.at[n])
-    wait(fin, own_sem)
-    wait(wg_out.at[:, pl.ds(0, (N - 1) * T)], out_recv.at[4])
-    wait(wg_out.at[:, pl.ds(0, (N - 1) * T)], out_send.at[4])
+    rest = wg_out.at[:, pl.ds(0, (N - 1) * T)]
+    expect('fin', fin, own_sem)
+    expect('out4', rest, out_recv.at[4])
+    expect('out4 sent', rest, out_send.at[4])
+
+    for name in list(expected):
+        wait(name)
+
+
+def settle(*refs):
+    sems = refs[10]
+    copies = [pltpu.make_async_copy(refs[n], refs[5 + n], sems.at[n]) for n in range(5)]
+    for copy in copies:
+        copy.start()
+    for copy in copies:
+        copy.wait()
 
 
 def shards(queries, keys, values, gates, out_grad, out_weight, time_bias, lengths, stamps):
     width = N * T
-    event = jax.ShapeDtypeStruct((T, width), BF16)
+    event = pltpu.VMEM((T, width), BF16)
     block = pltpu.VMEM((width, T), BF16)
     across16 = pltpu.VMEM((T, width), BF16)
     across32 = pltpu.VMEM((T, width), F32)
     hbm = pl.BlockSpec(memory_space=pl.ANY)
-    vmem = pl.BlockSpec(memory_space=pltpu.VMEM)
-    smem = pl.BlockSpec(memory_space=pltpu.SMEM)
-    return pl.pallas_call(
+    away = pl.BlockSpec(memory_space=pltpu.HBM)
+    outs = pl.pallas_call(
         kernel,
-        out_shape=(event, event, event, event, jax.ShapeDtypeStruct((16, width), F32)),
-        in_specs=[hbm, hbm, hbm, hbm, vmem, vmem, vmem, smem, vmem],
+        out_shape=(event, event, event, event, pltpu.VMEM((16, width), F32)),
+        in_specs=[hbm] * 9,
         out_specs=(hbm,) * 5,
         scratch_shapes=[
             block, block, block, block,
@@ -280,18 +345,36 @@
             pltpu.VMEM((NZ, 16, T), BF16),
             pltpu.VMEM((NZ, 16, T), BF16),
             pltpu.VMEM((16, T), F32),
+            pltpu.VMEM((T, width), F32), pltpu.VMEM((16, width), F32), pltpu.VMEM((8, T), BF16),
+            pltpu.SMEM((1, 4), jnp.int32), pltpu.VMEM((1, T), jnp.int32),
             pltpu.SemaphoreType.DMA((7,)),
             pltpu.SemaphoreType.DMA((7,)),
+            pltpu.SemaphoreType.DMA((14,)),
+            pltpu.SemaphoreType.DMA((14,)),
             pltpu.SemaphoreType.DMA((4,)),
             pltpu.SemaphoreType.DMA((4,)),
             pltpu.SemaphoreType.DMA((5,)),
             pltpu.SemaphoreType.DMA((5,)),
             pltpu.SemaphoreType.DMA,
+            pltpu.SemaphoreType.DMA((5,)),
         ],
         compiler_params=pltpu.CompilerParams(
             collective_id=0, has_side_effects=True, vmem_limit_bytes=48 * 1024 * 1024
         ),
-    )(queries, keys, values, gates, out_grad, out_weight, time_bias, lengths, stamps.reshape(1, T))
+    )(
+        *(
+            pltpu.with_memory_space_constraint(a, pltpu.HBM)
+            for a in (queries, keys, values, gates, out_grad, out_weight, time_bias.T, lengths, stamps.reshape(1, T))
+        )
+    )
+    return pl.pallas_call(
+        settle,
+        out_shape=[jax.ShapeDtypeStruct(o.shape, o.dtype) for o in outs],
+        in_specs=[hbm] * 5,
+        out_specs=[away] * 5,
+        scratch_shapes=[pltpu.SemaphoreType.DMA((5,))],
+        compiler_params=pltpu.CompilerParams(vmem_limit_bytes=4 * 1024 * 1024),
+    )(*(pltpu.with_memory_space_constraint(o, pltpu.VMEM) for o in outs))
 
 
 def solution(mesh):

time: 87.4 us -> 64.9 us (0.74)
  Pallas kernels: 76.4 us -> 64.1 us
  local copies, waits for them, and re-layouts: 9.93 us -> 0 us
    pallas_call x1 -> x2, Pallas kernels: 76.4 us -> 64.1 us  [the longest x1 63.1 us: shards(): pl.pallas_call(kernel, out_shape=(event, event, event, event, pltpu.VMEM(...]
    unnamed x22 -> x0, local copies, waits for them, and re-layouts: 9.93 us -> none
where the time goes in v2:
time: 64.9 us; the launch traced here: 64.7 us
  Pallas kernels  64.1 us (99%)
    pallas_call x1, Pallas kernels, shards(): pl.pallas_call(kernel, out_shape=(event, event, event, event, pltpu.VMEM(...  63.1 us

profile of v2, /device:TPU:1, one launch (start us, length us, event | category | flops | bytes accessed | tf_op | source)
XLA Modules:
  0.0 64.7 jit_solution(5008572153881423799)
XLA Ops:
  0.6 63.1 %shard_map.128 = (bf16[128,1024]{1,0:T(8,128)(2,1)S(1)}, bf16[128,1024]{1,0:T(8,128)(2,1)S(1)}, bf16[128,1024]{1,0:T(8,128)(2,1)S(1)}, bf16[128,1024]{1,0:T(8,128)(2,1)S(1)}, f32[16,1024]{1,0:T(8,128)S(1)}) custom-call(bf16[128,1024]{1,0:T(8,128)(2,1)} %q_in.1, bf16[128,1024]{1,0:T(8,128)(2,1)} %k_in.1, bf16[128,1024]{1,0:T(8,128)(2,1)} %v_in.1, ...), custom_call_target="tpu_custom_call" | custom-call | tf_op jit(solution)/shard_map/pallas_call | solution.py:325
  63.7 1.0 %shard_map.129 = (bf16[128,1024]{1,0:T(8,128)(2,1)}, bf16[128,1024]{1,0:T(8,128)(2,1)}, bf16[128,1024]{1,0:T(8,128)(2,1)}, bf16[128,1024]{1,0:T(8,128)(2,1)}, f32[16,1024]{1,0:T(8,128)}) custom-call(bf16[128,1024]{1,0:T(8,128)(2,1)S(1)} %get-tuple-element.10.refs_0_, bf16[128,1024]{1,0:T(8,128)(2,1)S(1)} %get-tuple-element.11.refs_1_, ...), custom_call_target="tpu_custom_call" | custom-call | tf_op jit(solution)/shard_map/pallas_call | solution.py:370

commit v3 on v2

v3 whole, which is shorter than its diff:
```python
import functools

import jax
import jax.numpy as jnp
from jax import lax
from jax.experimental import pallas as pl
from jax.experimental.pallas import tpu as pltpu
from jax.sharding import PartitionSpec as P

norm_eps = 1e-06
MESH = pl.DeviceIdType.MESH
F32 = jnp.float32
BF16 = jnp.bfloat16
T = 128
N = 8
NY = 4
NZ = 16
HUB = 11
BAND = 4
NT = (((1,), (1,)), ((), ()))


def rows(i):
    return pl.ds(i * T, T)


def dyn(i):
    return pl.ds(pl.multiple_of(i * T, T), T)


def kernel(
    q_in, k_in, v_in, g_in, og_hbm, w_hbm, tb_hbm, len_hbm, st_hbm,
    dq_out, dk_out, dv_out, dg_out, wg_out,
    q, k, v, g, og, w, stamps, stats, grad_stats,
    kt, vt, ngt, gt, at, dat, gated, normed, probs, slope, ds,
    dq, dk, dv, dg, wg, ry, zs, rz, fin,
    og_in, w_in, tb_in, len_in, st_in,
    in_send, in_recv, og_send, og_recv, w_send, w_recv, out_send, out_recv, own_sem, load_sem, ready,
):
    dp, me = lax.axis_index("dp"), lax.axis_index("seq")
    z, y = lax.div(dp, NY), lax.rem(dp, NY)
    chip, core = lax.div(me, 2), lax.rem(me, 2)
    left, right = lax.rem(me + N - 2, N), lax.rem(me + 2, N)
    facing = lax.rem(me + 4, N)
    sibling = 2 * chip + 1 - core
    width = N * T

    def seq_peer(s):
        return (dp, s)

    def z_peer(zz):
        return (zz * NY + y, me)

    def y_peer(yy):
        return (z * NY + yy, me)

    def send(src, dst, ssem, rsem, device):
        pltpu.make_async_remote_copy(
            src_ref=src, dst_ref=dst, send_sem=ssem, recv_sem=rsem, device_id=device, device_id_type=MESH
        ).start()

    def greet(first, last, sem, peer):
        def one(n, carry):
            pl.semaphore_signal(sem, inc=1, device_id=peer(n), device_id_type=MESH)
            return carry

        lax.fori_loop(first, last, one, 0)

    expected = {}

    def expect(name, ref, sem):
        expected[name] = (ref, sem)

    def wait(name):
        ref, sem = expected.pop(name)
        pltpu.make_async_copy(ref, ref, sem).wait()

    others = q.at[pl.ds(0, (N - 1) * T), :]

    def collect(n, src, dst):
        pltpu.make_async_copy(src.at[:, dyn(me)], dst.at[dyn(me), :], in_recv.at[n]).start()
        for d in range(1, N):
            peer = lax.rem(me + d, N)
            send(src.at[:, dyn(peer)], dst.at[dyn(me), :], in_send.at[n], in_recv.at[n], seq_peer(peer))

    def share(name, n, ref):
        for d in range(1, N):
            send(ref.at[me], ref.at[me], in_send.at[n], in_recv.at[n], seq_peer(lax.rem(me + d, N)))
        expect(name, ref.at[pl.ds(0, N - 1)], in_recv.at[n])
        expect(name + ' sent', ref.at[pl.ds(0, N - 1)], in_send.at[n])

    def deliver(name, n, src, dst):
        pltpu.make_async_copy(src.at[dyn(me), :], dst.at[:, dyn(me)], out_recv.at[n]).start()
        for d in range(1, N):
            peer = lax.rem(me + d, N)
            send(src.at[dyn(peer), :], dst.at[:, dyn(me)], out_send.at[n], out_recv.at[n], seq_peer(peer))
        expect(name, dst, out_recv.at[n])
        expect(name + ' sent', others, out_send.at[n])

    columns = [pl.ds(n * 2 * T, 2 * T) for n in range(4)]
    parts = [pl.ds(n * 4, 4) for n in range(4)]

    def pass_on(kind, n, owner, first, count, peer):
        ref = og.at[pl.ds(pl.multiple_of(owner * T + first, T // 2), count), columns[n]]
        send(ref, ref, og_send.at[4 * kind + n], og_recv.at[4 * kind + n], seq_peer(peer))

    def expect_part(kind, n, count):
        size = og.at[pl.ds(0, count), pl.ds(0, 2 * T)]
        expect('og%d-%d' % (kind, n), size, og_recv.at[4 * kind + n])
        expect('og%d-%d sent' % (kind, n), size, og_send.at[4 * kind + n])

    loads = [
        pltpu.make_async_copy(src, dst, load_sem.at[n])
        for n, (src, dst) in enumerate(
            ((og_hbm, og_in), (w_hbm, w_in), (tb_hbm, tb_in), (len_hbm, len_in), (st_hbm, st_in))
        )
    ]
    for load in loads:
        load.start()

    barrier = pltpu.get_barrier_semaphore()
    for d in range(1, N):
        pl.semaphore_signal(barrier, inc=1, device_id=seq_peer(lax.rem(me + d, N)), device_id_type=MESH)
    greet(y + 1, NY, barrier, y_peer)

    @pl.when(z != HUB)
    def _():
        pl.semaphore_signal(barrier, inc=1, device_id=z_peer(HUB), device_id_type=MESH)

    for load in loads:
        load.wait()
    og[dyn(me), :] = og_in[...].astype(BF16)
    stamps[me] = st_in[...]
    w[z, y] = w_in[:, dyn(me)].astype(BF16)

    pl.semaphore_wait(barrier, N - 1 + y + jnp.where(z == HUB, NZ - 1, 0))
    share('stamps', 0, stamps)
    collect(1, q_in, q)
    greet(0, y, ready, y_peer)

    @pl.when(z == HUB)
    def _():
        for d in range(1, NZ):
            pl.semaphore_signal(ready, inc=1, device_id=z_peer(lax.rem(z + d, NZ)), device_id_type=MESH)

    heads_of = tb_in[...].astype(F32)
    mine = jnp.where(lax.broadcasted_iota(jnp.int32, heads_of.shape, 0) == me, heads_of, 0.0)
    table = jnp.broadcast_to(jnp.sum(mine, axis=0, keepdims=True), (T, T))
    place = lax.broadcasted_iota(jnp.int32, (1, N * T), 1)
    end = jnp.int32(0)
    start = jnp.zeros((1, N * T), jnp.int32)
    for n in range(len_in.shape[1]):
        end = end + len_in[0, n]
        start = jnp.where(place >= end, end, start)
    below = lax.broadcasted_iota(jnp.int32, (T, T), 0)
    across = lax.broadcasted_iota(jnp.int32, (T, T), 1)
    def spread_weight():
        answers = NY - 1 - y + jnp.where(z == HUB, 0, 1)

        @pl.when(answers > 0)
        def _():
            pl.semaphore_wait(ready, answers)

        for d in range(1, NZ):
            send(w.at[z, y], w.at[z, y], w_send.at[0], w_recv.at[0], z_peer(lax.rem(z + d, NZ)))

    def start_ring():
        pass_on(0, 0, me, 0, T, right)
        pass_on(1, 0, me, 0, T, left)
        pass_on(5, 0, me, 0, T, facing)
        pass_on(2, 0, me, 0, T, sibling)

    @pl.when(z < NZ // 4)
    def _():
        collect(2, k_in, k)
        collect(3, v_in, v)
        collect(4, g_in, g)
        start_ring()

    @pl.when((z >= NZ // 4) & (z < NZ // 2))
    def _():
        collect(2, k_in, k)
        collect(3, v_in, v)
        spread_weight()
        collect(4, g_in, g)
        start_ring()

    @pl.when(z >= NZ // 2)
    def _():
        collect(2, k_in, k)
        spread_weight()
        collect(3, v_in, v)
        collect(4, g_in, g)
        start_ring()

    for n, (name, dst) in enumerate((('q', q), ('k', k), ('v', v), ('g', g))):
        expect(name, dst, in_recv.at[1 + n])
        expect(name + ' sent', others, in_send.at[1 + n])
    for kind in (0, 1, 5, 2):
        expect_part(kind, 0, T)
    expect('w z', w.at[pl.ds(0, NZ - 1), 0], w_recv.at[0])
    expect('w z sent', w.at[pl.ds(0, NZ - 1), 0], w_send.at[0])

    wait('stamps')
    wait('q')
    wait('k')
    for i in range(N):
        query_stamps = stamps[i, 0:1, :]
        for j in range(max(0, i - BAND), i + 1):
            key_stamps = jnp.transpose(jnp.broadcast_to(stamps[j, 0:1, :], (T, T)))
            bucket = jnp.clip(query_stamps - key_stamps, 0, T - 1)
            bias = jnp.take_along_axis(table, bucket, axis=1)
            score = lax.dot_general(k[rows(j), :], q[rows(i), :], NT, preferred_element_type=F32) + bias
            allowed = below >= start[:, i * T : (i + 1) * T] - j * T
            if i == j:
                allowed = allowed & (below <= across)
            sigma = jnp.where(allowed, 0.5 * jnp.tanh(0.5 * score) + 0.5, 0.0)
            prob = score * sigma
            probs[rows(j), rows(i)] = prob.astype(BF16)
            slope[rows(j), rows(i)] = sigma + prob * (1.0 - sigma)

    wait('v')
    for i in range(N):
        vt[:, rows(i)] = jnp.transpose(v[rows(i), :])
        kt[:, rows(i)] = jnp.transpose(k[rows(i), :])

    def put(ref, n, i, value):
        row, col = 4 * n + i // 2, (i % 2) * T
        ref[me, row : row + 1, col : col + T] = value

    def get(ref, n, i):
        row, col = 4 * n + i // 2, (i % 2) * T
        return ref[:, row, col : col + T]

    for i in range(N):
        lo, hi = max(0, i - BAND) * T, (i + 1) * T
        attended = jnp.dot(vt[:, lo:hi], probs[lo:hi, rows(i)], preferred_element_type=F32)
        at[:, rows(i)] = attended
        mean = jnp.sum(attended, axis=0, keepdims=True) * (1.0 / T)
        centred = attended - mean
        put(stats, 0, i, mean)
        put(stats, 1, i, jnp.sum(centred * centred, axis=0, keepdims=True))
    share('stats', 5, stats)
    pl.when(z < NZ // 4)(spread_weight)
    for n in range(1, 4):
        pass_on(0, n, me, 0, T, right)
        expect_part(0, n, T)
        pass_on(1, n, me, 0, T, left)
        expect_part(1, n, T)
        pass_on(2, n, me, 0, T, sibling)
        expect_part(2, n, T)

    wait('og0-0')
    pass_on(3, 0, left, 0, T, sibling)
    expect_part(3, 0, T)
    wait('og1-0')
    pass_on(4, 0, right, 0, T, sibling)
    expect_part(4, 0, T)
    wait('og5-0')
    pass_on(7, 0, facing, 0, T, sibling)
    expect_part(7, 0, T)

    wait('stats')
    inverses = []
    for i in range(N):
        means = get(stats, 0, i)
        mean = jnp.sum(means, axis=0, keepdims=True) * (1.0 / N)
        apart = means - mean
        spread = jnp.sum(get(stats, 1, i), axis=0, keepdims=True) + T * jnp.sum(apart * apart, axis=0, keepdims=True)
        inverse = lax.rsqrt(spread * (1.0 / width) + norm_eps)
        inverses.append(inverse)
        normed_tile = (at[:, rows(i)] - mean) * inverse
        at[:, rows(i)] = normed_tile
        normed[rows(i), :] = jnp.transpose(normed_tile)

    wait('g')
    for i in range(N):
        gate = jnp.transpose(g[rows(i), :].astype(F32))
        gt[:, rows(i)] = gate
        gated[:, rows(i)] = (at[:, rows(i)] * gate).astype(BF16)

    def weight_part(n):
        terms = jnp.dot(gated[...], og[:, columns[n]], preferred_element_type=F32)
        for i in range(2):
            block = jnp.transpose(terms[:, i * T : (i + 1) * T]).astype(BF16)
            wg[4 * n + 2 * i : 4 * n + 2 * i + 2] = block.reshape(2, NY, 16, T)
        ry[y, parts[n]] = wg[parts[n], y]
        for d in range(1, NY):
            yy = lax.rem(y + d, NY)
            send(wg.at[parts[n], yy], ry.at[y, parts[n]], w_send.at[2 + n], w_recv.at[2 + n], y_peer(yy))
        part_of = ry.at[pl.ds(0, NY - 1), parts[n]]
        expect('ry%d' % n, part_of, w_recv.at[2 + n])
        expect('ry%d sent' % n, part_of, w_send.at[2 + n])

    for kind in (2, 3, 4, 7):
        wait('og%d-0' % kind)
    weight_part(0)
    wait('w z')
    for d in range(1, NY):
        send(w.at[:, y], w.at[:, y], w_send.at[1], w_recv.at[1], y_peer(lax.rem(y + d, NY)))
    expect('w y', w.at[:, pl.ds(0, NY - 1)], w_recv.at[1])
    expect('w y sent', w.at[:, pl.ds(0, NY - 1)], w_send.at[1])
    for n in range(1, 4):
        wait('og0-%d' % n)
        pass_on(5, n, left, 0, T // 2, right)
        expect_part(5, n, T // 2)
        wait('og1-%d' % n)
        pass_on(6, n, right, T // 2, T // 2, left)
        expect_part(6, n, T // 2)
        pass_on(3, n, left, 0, T, sibling)
        expect_part(3, n, T)
        pass_on(4, n, right, 0, T, sibling)
        expect_part(4, n, T)
    for n in range(1, 4):
        wait('og5-%d' % n)
        pass_on(7, n, facing, 0, T // 2, sibling)
        expect_part(7, n, T // 2)
        wait('og6-%d' % n)
        pass_on(8, n, facing, T // 2, T // 2, sibling)
        expect_part(8, n, T // 2)
        for kind in (2, 3, 4, 7, 8):
            wait('og%d-%d' % (kind, n))
        weight_part(n)

    wait('w y')
    weight = w[...].reshape(width, T)
    for i in range(N):
        gated_grad = jnp.dot(og[rows(i), :], weight, preferred_element_type=F32)
        dg[rows(i), :] = (gated_grad * normed[rows(i), :]).astype(BF16)
        normed_grad = jnp.transpose(gated_grad) * gt[:, rows(i)]
        ngt[:, rows(i)] = normed_grad
        put(grad_stats, 0, i, jnp.sum(normed_grad, axis=0, keepdims=True))
        put(grad_stats, 1, i, jnp.sum(normed_grad * at[:, rows(i)], axis=0, keepdims=True))
    share('grad stats', 6, grad_stats)

    for n, part in enumerate(parts):
        wait('ry%d' % n)
        total = ry[0, part].astype(F32)
        for m in range(1, NY):
            total = total + ry[m, part].astype(F32)
        zs[part] = total.astype(BF16)
        for d in range(4):
            zz = 4 * n + lax.rem(z + d, 4)

            @pl.when(zz != z)
            def _():
                send(zs.at[zz], rz.at[z], w_send.at[6], w_recv.at[6], z_peer(zz))

    rz[z] = zs[z]
    expect('rz', rz.at[pl.ds(0, NZ - 1)], w_recv.at[6])
    expect('rz sent', rz.at[pl.ds(0, NZ - 1)], w_send.at[6])
    deliver('dg', 0, dg, dg_out)

    wait('grad stats')
    for i in range(N):
        grad_mean = jnp.sum(get(grad_stats, 0, i), axis=0, keepdims=True) * (1.0 / width)
        cross = jnp.sum(get(grad_stats, 1, i), axis=0, keepdims=True) * (1.0 / width)
        dat[:, rows(i)] = (inverses[i] * (ngt[:, rows(i)] - grad_mean - at[:, rows(i)] * cross)).astype(BF16)

    for j in range(N):
        lo, hi = j * T, min(j + BAND + 1, N) * T
        dv[rows(j), :] = lax.dot_general(
            probs[rows(j), lo:hi], dat[:, lo:hi], NT, preferred_element_type=F32
        ).astype(BF16)
    deliver('dv', 1, dv, dv_out)
    for i in range(N):
        lo, hi = max(0, i - BAND) * T, (i + 1) * T
        for j in range(max(0, i - BAND), i + 1):
            prob_grad = jnp.dot(v[rows(j), :], dat[:, rows(i)], preferred_element_type=F32)
            ds[rows(j), rows(i)] = (prob_grad * slope[rows(j), rows(i)]).astype(BF16)
        dq[rows(i), :] = jnp.transpose(
            jnp.dot(kt[:, lo:hi], ds[lo:hi, rows(i)], preferred_element_type=F32)
        ).astype(BF16)
    deliver('dq', 2, dq, dq_out)

    for j in range(N):
        lo, hi = j * T, min(j + BAND + 1, N) * T
        dk[rows(j), :] = jnp.dot(ds[rows(j), lo:hi], q[lo:hi, :], preferred_element_type=F32).astype(BF16)
    deliver('dk', 3, dk, dk_out)

    for name in list(expected):
        if name[:2] not in ('dv', 'dq', 'dk', 'rz'):
            wait(name)
    wait('rz')
    total = rz[0].astype(F32)
    for n in range(1, NZ):
        total = total + rz[n].astype(F32)
    fin[...] = total * (1.0 / T)
    pltpu.make_async_copy(fin, wg_out.at[:, dyn(me)], own_sem).start()
    for d in range(1, N):
        send(fin, wg_out.at[:, dyn(me)], out_send.at[4], out_recv.at[4], seq_peer(lax.rem(me + d, N)))
    rest = wg_out.at[:, pl.ds(0, (N - 1) * T)]
    expect('fin', fin, own_sem)
    expect('dw', rest, out_recv.at[4])
    expect('dw sent', rest, out_send.at[4])

    for name in list(expected):
        wait(name)


def settle(*refs):
    sems = refs[10]
    copies = [pltpu.make_async_copy(refs[n], refs[5 + n], sems.at[n]) for n in range(5)]
    for copy in copies:
        copy.start()
    for copy in copies:
        copy.wait()


def shards(queries, keys, values, gates, out_grad, out_weight, time_bias, lengths, stamps):
    width = N * T
    event = pltpu.VMEM((T, width), BF16)
    block = pltpu.VMEM((width, T), BF16)
    across16 = pltpu.VMEM((T, width), BF16)
    across32 = pltpu.VMEM((T, width), F32)
    hbm = pl.BlockSpec(memory_space=pl.ANY)
    away = pl.BlockSpec(memory_space=pltpu.HBM)
    outs = pl.pallas_call(
        kernel,
        out_shape=(event, event, event, event, pltpu.VMEM((16, width), F32)),
        in_specs=[hbm] * 9,
        out_specs=(hbm,) * 5,
        scratch_shapes=[
            block, block, block, block,
            pltpu.VMEM((width, width), BF16),
            pltpu.VMEM((NZ, NY, 16, T), BF16),
            pltpu.VMEM((N, 1, T), jnp.int32),
            pltpu.VMEM((N, 8, 2 * T), F32), pltpu.VMEM((N, 8, 2 * T), F32),
            across16, across16,
            across32, across32, across32,
            across16, across16,
            pltpu.VMEM((width, T), F32),
            pltpu.VMEM((width, width), BF16),
            pltpu.VMEM((width, width), F32),
            pltpu.VMEM((width, width), BF16),
            block, block, block, block,
            pltpu.VMEM((NZ, NY, 16, T), BF16),
            pltpu.VMEM((NY, NZ, 16, T), BF16),
            pltpu.VMEM((NZ, 16, T), BF16),
            pltpu.VMEM((NZ, 16, T), BF16),
            pltpu.VMEM((16, T), F32),
            pltpu.VMEM((T, width), F32), pltpu.VMEM((16, width), F32), pltpu.VMEM((8, T), BF16),
            pltpu.SMEM((1, 4), jnp.int32), pltpu.VMEM((1, T), jnp.int32),
            pltpu.SemaphoreType.DMA((7,)),
            pltpu.SemaphoreType.DMA((7,)),
            pltpu.SemaphoreType.DMA((36,)),
            pltpu.SemaphoreType.DMA((36,)),
            pltpu.SemaphoreType.DMA((7,)),
            pltpu.SemaphoreType.DMA((7,)),
            pltpu.SemaphoreType.DMA((5,)),
            pltpu.SemaphoreType.DMA((5,)),
            pltpu.SemaphoreType.DMA,
            pltpu.SemaphoreType.DMA((5,)),
            pltpu.SemaphoreType.REGULAR,
        ],
        compiler_params=pltpu.CompilerParams(
            collective_id=0, has_side_effects=True, vmem_limit_bytes=48 * 1024 * 1024
        ),
    )(
        *(
            pltpu.with_memory_space_constraint(a, pltpu.HBM)
            for a in (queries, keys, values, gates, out_grad, out_weight, time_bias.T, lengths, stamps.reshape(1, T))
        )
    )
    return pl.pallas_call(
        settle,
        out_shape=[jax.ShapeDtypeStruct(o.shape, o.dtype) for o in outs],
        in_specs=[hbm] * 5,
        out_specs=[away] * 5,
        scratch_shapes=[pltpu.SemaphoreType.DMA((5,))],
        compiler_params=pltpu.CompilerParams(vmem_limit_bytes=4 * 1024 * 1024),
    )(*(pltpu.with_memory_space_constraint(o, pltpu.VMEM) for o in outs))


def solution(mesh):
    events = P(("dp", "seq"), None)
    return jax.shard_map(
        shards,
        mesh=mesh,
        in_specs=(
            events, events, events, events, events, P("dp", None), P(), P("dp", None), P(("dp", "seq")),
        ),
        out_specs=(events, events, events, events, P("dp", None)),
        check_vma=False,
    )
```

time: 64.9 us -> 55.6 us (0.86)
  Pallas kernels: 64.1 us -> 54.8 us
    pallas_call x1, Pallas kernels: 63.1 us -> 53.8 us  [shards(): pl.pallas_call(kernel, out_shape=(event, event, event, event, pltpu.VMEM(...]
where the time goes in v3:
time: 55.6 us; the launch traced here: 55.5 us
  Pallas kernels  54.8 us (99%)
  between operations  0.64 us (1%)
    pallas_call x1, Pallas kernels, shards(): pl.pallas_call(kernel, out_shape=(event, event, event, event, pltpu.VMEM(...  53.8 us

profile of v3, /device:TPU:1, one launch (start us, length us, event | category | flops | bytes accessed | tf_op | source)
XLA Modules:
  0.0 55.5 jit_solution(6687915017352572515)
XLA Ops:
  0.6 53.8 %shard_map.128 = (bf16[128,1024]{1,0:T(8,128)(2,1)S(1)}, bf16[128,1024]{1,0:T(8,128)(2,1)S(1)}, bf16[128,1024]{1,0:T(8,128)(2,1)S(1)}, bf16[128,1024]{1,0:T(8,128)(2,1)S(1)}, f32[16,1024]{1,0:T(8,128)S(1)}) custom-call(bf16[128,1024]{1,0:T(8,128)(2,1)} %q_in.1, bf16[128,1024]{1,0:T(8,128)(2,1)} %k_in.1, bf16[128,1024]{1,0:T(8,128)(2,1)} %v_in.1, ...), custom_call_target="tpu_custom_call" | custom-call | tf_op jit(solution)/shard_map/pallas_call | solution.py:418
  54.4 1.0 %shard_map.129 = (bf16[128,1024]{1,0:T(8,128)(2,1)}, bf16[128,1024]{1,0:T(8,128)(2,1)}, bf16[128,1024]{1,0:T(8,128)(2,1)}, bf16[128,1024]{1,0:T(8,128)(2,1)}, f32[16,1024]{1,0:T(8,128)}) custom-call(bf16[128,1024]{1,0:T(8,128)(2,1)S(1)} %get-tuple-element.10.refs_0_, bf16[128,1024]{1,0:T(8,128)(2,1)S(1)} %get-tuple-element.11.refs_1_, ...), custom_call_target="tpu_custom_call" | custom-call | tf_op jit(solution)/shard_map/pallas_call | solution.py:465

commit v4 on v3

--- a/solution.py
+++ b/solution.py
@@ -289,7 +289,6 @@
             yy = lax.rem(y + d, NY)
             send(wg.at[parts[n], yy], ry.at[y, parts[n]], w_send.at[2 + n], w_recv.at[2 + n], y_peer(yy))
         part_of = ry.at[pl.ds(0, NY - 1), parts[n]]
-        expect('ry%d' % n, part_of, w_recv.at[2 + n])
         expect('ry%d sent' % n, part_of, w_send.at[2 + n])
 
     for kind in (2, 3, 4, 7):
@@ -311,6 +310,24 @@
         expect_part(3, n, T)
         pass_on(4, n, right, 0, T, sibling)
         expect_part(4, n, T)
+    def sum_part(n):
+        landed = ry.at[pl.ds(0, NY - 1), parts[n]]
+        pltpu.make_async_copy(landed, landed, w_recv.at[2 + n]).wait()
+        total = ry[0, parts[n]].astype(F32)
+        for m in range(1, NY):
+            total = total + ry[m, parts[n]].astype(F32)
+        zs[parts[n]] = total.astype(BF16)
+        for d in range(4):
+            zz = 4 * n + lax.rem(z + d, 4)
+
+            @pl.when(zz != z)
+            def _():
+                send(zs.at[zz], rz.at[z], w_send.at[6], w_recv.at[6], z_peer(zz))
+
+    @pl.when(z >= NZ // 4)
+    def _():
+        sum_part(0)
+
     for n in range(1, 4):
         wait('og5-%d' % n)
         pass_on(7, n, facing, 0, T // 2, sibling)
@@ -333,23 +350,21 @@
         put(grad_stats, 1, i, jnp.sum(normed_grad * at[:, rows(i)], axis=0, keepdims=True))
     share('grad stats', 6, grad_stats)
 
-    for n, part in enumerate(parts):
-        wait('ry%d' % n)
-        total = ry[0, part].astype(F32)
-        for m in range(1, NY):
-            total = total + ry[m, part].astype(F32)
-        zs[part] = total.astype(BF16)
-        for d in range(4):
-            zz = 4 * n + lax.rem(z + d, 4)
-
-            @pl.when(zz != z)
-            def _():
-                send(zs.at[zz], rz.at[z], w_send.at[6], w_recv.at[6], z_peer(zz))
+    @pl.when(z >= NZ // 4)
+    def _():
+        for n in range(1, 4):
+            sum_part(n)
+
+    deliver('dg', 0, dg, dg_out)
+
+    @pl.when(z < NZ // 4)
+    def _():
+        for n in range(4):
+            sum_part(n)
 
     rz[z] = zs[z]
     expect('rz', rz.at[pl.ds(0, NZ - 1)], w_recv.at[6])
     expect('rz sent', rz.at[pl.ds(0, NZ - 1)], w_send.at[6])
-    deliver('dg', 0, dg, dg_out)
 
     wait('grad stats')
     for i in range(N):
@@ -362,6 +377,7 @@
         dv[rows(j), :] = lax.dot_general(
             probs[rows(j), lo:hi], dat[:, lo:hi], NT, preferred_element_type=F32
         ).astype(BF16)
+
     deliver('dv', 1, dv, dv_out)
     for i in range(N):
         lo, hi = max(0, i - BAND) * T, (i + 1) * T

time: 55.6 us -> 55.6 us (level)
  no operation moved by 1% of the time
where the time goes in v4:
time: 55.6 us; the launch traced here: 55.5 us
  Pallas kernels  54.8 us (99%)
  between operations  0.64 us (1%)
    pallas_call x1, Pallas kernels, shards(): pl.pallas_call(kernel, out_shape=(event, event, event, event, pltpu.VMEM(...  53.8 us

profile of v4, /device:TPU:1, one launch (start us, length us, event | category | flops | bytes accessed | tf_op | source)
XLA Modules:
  0.0 55.5 jit_solution(10490475378201288317)
XLA Ops:
  0.6 53.8 %shard_map.128 = (bf16[128,1024]{1,0:T(8,128)(2,1)S(1)}, bf16[128,1024]{1,0:T(8,128)(2,1)S(1)}, bf16[128,1024]{1,0:T(8,128)(2,1)S(1)}, bf16[128,1024]{1,0:T(8,128)(2,1)S(1)}, f32[16,1024]{1,0:T(8,128)S(1)}) custom-call(bf16[128,1024]{1,0:T(8,128)(2,1)} %q_in.1, bf16[128,1024]{1,0:T(8,128)(2,1)} %k_in.1, bf16[128,1024]{1,0:T(8,128)(2,1)} %v_in.1, ...), custom_call_target="tpu_custom_call" | custom-call | tf_op jit(solution)/shard_map/pallas_call | solution.py:434
  54.4 1.0 %shard_map.129 = (bf16[128,1024]{1,0:T(8,128)(2,1)}, bf16[128,1024]{1,0:T(8,128)(2,1)}, bf16[128,1024]{1,0:T(8,128)(2,1)}, bf16[128,1024]{1,0:T(8,128)(2,1)}, f32[16,1024]{1,0:T(8,128)}) custom-call(bf16[128,1024]{1,0:T(8,128)(2,1)S(1)} %get-tuple-element.10.refs_0_, bf16[128,1024]{1,0:T(8,128)(2,1)S(1)} %get-tuple-element.11.refs_1_, ...), custom_call_target="tpu_custom_call" | custom-call | tf_op jit(solution)/shard_map/pallas_call | solution.py:481
